TPU v7x, 128 devices: a whole 4x4x4 slice. The times are simulated.
128 devices in a mesh: ctx: 16 (over y, x), ch: 8 (over z, core).
Axes of the slice: x: 4, y: 4, z: 4, core: 2. Of those that a mesh axis runs over, the one named last changes fastest.
Arguments:
- tokens: bfloat16 [8192, 8192], P('ctx', 'ch'), may hold values from -6 to 6
- in_weight: bfloat16 [8192, 3, 4096], P('ch', None, 'ctx'), may hold values from -0.09375 to 0.09375
- short_taps: float32 [7, 3, 4096], P(None, None, 'ch'), may hold values from -2 to 2
- residues: float32 [16, 4096], P(None, 'ch'), may hold values from -1.5 to 1.5
- decay_scale: float32 [16, 4096], P(None, 'ch'), may hold values from 0.2 to 512, as said below
- skip_gain: float32 [4096], P('ch'), may hold values from -4 to 4
Outputs:
- filtered: bfloat16 [8192, 4096], P('ctx', 'ch')
Inputs may be any that keep to these rules, and one draw needn't show every extreme that they name: decay_scale[r, c] / 8192 is the fraction by which mode r of channel c fades per position.
All inputs are finite; a program needn't handle non-finite values.
Results may differ from a plain program's by a relative error of at most 0.035.
Values may be sent and summed in bfloat16 or wider, within the bound.
No kernel may reach another device: no remote copies, remote signals or barrier semaphores. Data moves between devices by JAX's collectives and lax.ppermute only.
A program may use at most 128 MiB of HBM per device.

v0:
```python
import math
import jax
import jax.numpy as jnp
from jax import lax
from jax.sharding import PartitionSpec as P

SHORT = 7


def passed_along(value, axis, steps):
    count = lax.axis_size(axis)
    initial, last = (max(0, -steps), min(count, count - steps))
    return lax.ppermute(value, axis, [(source, source + steps) for source in range(initial, last)])


def on_device(tokens, in_weight, short_taps, residues, decay_scale, skip_gain):
    length = tokens.shape[0]
    partial_value = jnp.einsum(
        "td,dmg->tmg",
        tokens,
        lax.all_gather(in_weight, "ctx", axis=2, tiled=True),
        preferred_element_type=jnp.float32,
    )
    projected = lax.psum_scatter(
        partial_value.astype(jnp.bfloat16), "ch", scatter_dimension=2, tiled=True
    )
    previous = passed_along(projected[length - (SHORT - 1) :], "ctx", 1)
    extended = jnp.concatenate([previous, projected], axis=0).astype(jnp.float32)
    smoothed = short_taps[0] * extended[SHORT - 1 : SHORT - 1 + length]
    for offset in range(1, SHORT):
        smoothed = (
            smoothed
            + short_taps[offset] * extended[SHORT - 1 - offset : SHORT - 1 - offset + length]
        )
    gate_part = smoothed[:, 0, :]
    source = smoothed[:, 1, :] * smoothed[:, 2, :]
    channels = source.shape[1]
    seq_total = length * lax.axis_size("ctx")
    decay_rate = decay_scale / seq_total
    mode_weight = residues * jnp.sqrt(-jnp.expm1(-2.0 * decay_rate))
    offsets = jnp.arange(length, dtype=jnp.float32)
    fading = jnp.exp(-decay_rate[:, None, :] * offsets[None, :, None])
    kernel = jnp.sum(fading * mode_weight[:, None, :], axis=0)
    highest = lax.Precision.HIGHEST
    block_len = math.gcd(length, 64)
    block_count = length // block_len
    pieces = source.reshape(block_count, block_len, channels)
    lag_steps = (
        jnp.arange(block_len, dtype=jnp.int32)[:, None]
        - jnp.arange(block_len, dtype=jnp.int32)[None, :]
    )
    toeplitz = jnp.where((lag_steps >= 0)[:, :, None], kernel[jnp.maximum(lag_steps, 0)], 0.0)
    within = jnp.einsum("tsc,jsc->jtc", toeplitz, pieces, precision=highest)
    block_steps = jnp.arange(block_len, dtype=jnp.float32)
    closing = jnp.exp(-decay_rate[:, None, :] * (block_len - 1.0 - block_steps)[None, :, None])
    block_ends = jnp.einsum("rsc,jsc->jrc", closing, pieces, precision=highest)
    block_ids = jnp.arange(block_count, dtype=jnp.int32)
    block_gap = block_ids[:, None] - 1 - block_ids[None, :]
    gap_float = jnp.maximum(block_gap, 0).astype(jnp.float32)
    passing = jnp.exp(-(decay_rate * block_len)[None, None, :, :] * gap_float[:, :, None, None])
    passing = jnp.where((block_gap >= 0)[:, :, None, None], passing, 0.0)
    block_starts = jnp.einsum("jirc,irc->jrc", passing, block_ends, precision=highest)
    opening = jnp.exp(-decay_rate[:, None, :] * (block_steps + 1.0)[None, :, None])
    within = within + jnp.einsum(
        "rtc,jrc->jtc", opening, mode_weight[None, :, :] * block_starts, precision=highest
    )
    local_conv = within.reshape(length, channels)
    tail_decay = jnp.exp(-decay_rate[:, None, :] * (length - 1.0 - offsets)[None, :, None])
    end_state = jnp.sum(tail_decay * source[None, :, :], axis=1)
    states = lax.all_gather(end_state[None].astype(jnp.bfloat16), "ctx", axis=0, tiled=True).astype(
        jnp.float32
    )
    position = lax.axis_index("ctx")
    earlier_ids = jnp.arange(states.shape[0], dtype=jnp.int32)
    distance = jnp.maximum(position - 1 - earlier_ids, 0).astype(jnp.float32)
    weights = jnp.exp(-(decay_rate * length)[None, :, :] * distance[:, None, None])
    weights = jnp.where((earlier_ids < position)[:, None, None], weights, 0.0)
    incoming = jnp.sum(weights * states, axis=0)
    lead_decay = jnp.exp(-decay_rate[:, None, :] * (offsets + 1.0)[None, :, None])
    carried = jnp.sum(lead_decay * (mode_weight * incoming)[:, None, :], axis=0)
    convolved = local_conv + carried
    return (gate_part * (convolved + skip_gain[None, :] * source)).astype(jnp.bfloat16)


def solution(mesh):
    return jax.shard_map(
        on_device,
        mesh=mesh,
        in_specs=(
            P("ctx", "ch"),
            P("ch", None, "ctx"),
            P(None, None, "ch"),
            P(None, "ch"),
            P(None, "ch"),
            P("ch"),
        ),
        out_specs=P("ctx", "ch"),
        check_vma=False,
    )
```

profile of v0, /device:TPU:0, one launch (start us, length us, event | category | flops | bytes accessed | tf_op | source)
XLA Modules:
  0.0 418.5 jit_solution(9464340326151091559)
XLA Ops:
  6.5 0.0 copy-start
  6.5 0.0 all-gather.3.cloned.1.call-start
  6.5 0.7 all-gather.3.cloned.1.call-update
  7.3 0.0 reduce-scatter.2.cloned.1.call-start
  7.3 168.3 %all-gather.3.cloned.1.call-done = bf16[1024,3,4096]{2,0,1:T(8,128)(2,1)} async-done(((bf16[1024,3,256]{2,0,1:T(8,128)(2,1)}), bf16[1024,3,4096]{2,0,1:T(8,128)(2,1)}) %all-gather.3.cloned.1.call-update) | async-done | bytes 25165840 | tf_op jit(solution)/shard_map/all_gather | solution.py:21
  175.6 0.0 copy-done
  175.6 23.7 %convolution_convert_fusion = bf16[512,3,4096]{2,0,1:T(8,128)(2,1)} fusion(bf16[1024,3,4096]{2,0,1:T(8,128)(2,1)} %all-gather.3.cloned.1.call-done, bf16[512,1024]{1,0:T(8,128)(2,1)S(1)} %copy-done), kind=kOutput, calls=%fused_computation.6 | convolution fusion | flops 12891193344 | bytes 38797312 | tf_op jit(solution)/shard_map/td,dmg->tmg/dot_general | solution.py:18
  199.3 0.0 copy-start.6
  199.3 0.0 copy-start.5
  199.3 0.0 reduce-scatter.2.cloned.1.call-update
  199.3 0.1 reshape.140
  199.5 0.6 fusion.35
  200.1 0.1 maximum_convert_fusion.1
  200.2 0.0 copy-done.6
  200.3 0.0 copy-done.5
  200.3 71.2 %reduce-scatter.2.cloned.1.call-done = bf16[512,3,512]{2,0,1:T(8,128)(2,1)} async-done(((bf16[512,3,4096]{2,0,1:T(8,128)(2,1)}), bf16[512,3,512]{2,0,1:T(8,128)(2,1)}) %reduce-scatter.2.cloned.1.call-update) | async-done | bytes 1572880 | tf_op jit(solution)/shard_map/reduce_scatter | solution.py:24
  271.5 0.7 slice.74
  272.3 3.4 collective-permute-start
  275.7 0.1 copy.20
  275.8 1.3 collective-permute-done
  277.2 1.9 maximum_convert_fusion
  279.1 2.6 fusion.10
  281.7 0.0 copy-start.2
  281.7 0.2 fusion.42
  281.9 0.2 slice_multiply_fusion.7
  282.1 1.3 copy-done.2
  283.4 2.9 multiply_reduce_fusion.1
  286.3 28.4 %all-gather = bf16[256,512]{1,0:T(8,128)(2,1)} all-gather(bf16[16,512]{1,0:T(8,128)(2,1)S(1)} %multiply_reduce_fusion.1), channel_id=2, replica_groups=mesh['ctx'=16,'ch'=8] {'ctx'}, dimensions={0}, use_global_device_ids=true | all-gather | bytes 278528 | tf_op jit(solution)/shard_map/all_gather | solution.py:70
  314.7 0.8 copy.18
  315.5 1.1 fusion.34
  316.6 1.4 fusion.37
  318.0 0.8 copy.19
  318.9 7.8 %multiply_reduce_fusion.2 = (f32[512,512]{1,0:T(8,128)S(1)}, f32[512,512]{1,0:T(8,128)}) fusion(f32[16,512]{1,0:T(8,128)S(1)} %get-tuple-element.8, f32[16,512]{1,0:T(8,128)S(1)} %get-tuple-element.18, f32[16,512]{1,0:T(8,128)} %get-tuple-element.7, f32[512]{0:T(512)S(1)} %iota_add_fusion), kind=kLoop, calls=%fused_computation.5 | loop fusion | flops 24641536 | bytes 2197504 | tf_op jit(solution)/shard_map/reduce_sum | solution.py:43
  326.7 16.8 %gather_fusion = f32[4096,512]{1,0:T(8,128)} fusion(f32[512,512]{1,0:T(8,128)S(1)} %get-tuple-element.5, s32[4096]{0:T(1024)S(1)} %broadcast_clamp_fusion), kind=kCustom, calls=%fused_computation | custom fusion | bytes 16793600 | tf_op jit(solution)/shard_map/gather | solution.py:52
  343.5 16.3 %copy.17 = f32[64,64,512]{1,0,2:T(8,128)} copy(f32[64,64,512]{2,1,0:T(8,128)} %bitcast.55) | data formatting | bytes 16777216 | tf_op jit(solution)/shard_map/gather | solution.py:52
  359.8 0.0 copy-start.7
  359.8 0.0 copy-start.9
  359.8 8.3 %fusion.22 = f32[16,512,8]{0,2,1:T(8,128)} fusion(f32[8,64,512]{1,0,2:T(8,128)S(1)} %copy.18, f32[64]{0:T(128)S(1)} %iota_subtract_fusion.2, f32[16,512]{0,1:T(8,128)S(1)} %copy.20), kind=kOutput, calls=%fused_computation.36 | convolution fusion | flops 50855936 | bytes 1343744 | tf_op jit(solution)/shard_map/rsc,jsc->jrc/dot_general | solution.py:56
  368.1 2.2 copy.38
  370.2 0.0 copy-done.7
  370.2 0.0 copy-done.9
  370.2 0.5 multiply_reduce_fusion.3
  370.8 2.0 copy.30
  372.8 0.0 copy-start.3
  372.8 0.0 copy-start.4
  372.8 29.1 %fusion = f32[512,8,64]{2,1,0:T(8,128)S(1)} fusion(f32[8,64,512]{1,0,2:T(8,128)S(1)} %copy.18, f32[64,64,512]{1,0,2:T(8,128)} %copy.17, pred[64,64]{1,0:T(8,128)(4,1)S(1)} %subtract_compare_fusion), kind=kOutput, calls=%fused_computation.3 | convolution fusion | flops 203423744 | bytes 10489856 | tf_op jit(solution)/shard_map/tsc,jsc->jtc/dot_general | solution.py:53
  401.9 0.0 copy-done.3
  401.9 0.0 copy-done.4
  401.9 4.2 add_bitcast_fusion
  406.1 0.0 copy-start.8
  406.1 0.0 copy-start.1
  406.1 1.7 copy.22
  407.8 0.0 copy-done.8
  407.8 3.9 fusion.30
  411.7 0.0 copy-done.1
  (16 shorter events, 0.1 us)
Async XLA Ops:
  6.5 169.1 %copy-start = (bf16[512,1024]{1,0:T(8,128)(2,1)S(1)}, bf16[512,1024]{1,0:T(8,128)(2,1)}, u32[]{:S(2)}) copy-start(bf16[512,1024]{1,0:T(8,128)(2,1)} %param.6) | copy-start | bytes 3145732
  6.5 169.1 %all-gather.3.cloned.1.call-start = ((), (), s32[]{:S(2)}) async-start(), calls=%async_computation.1 | async-start | bytes 26738688 | tf_op jit(solution)/shard_map/all_gather | solution.py:21
  7.3 264.3 %reduce-scatter.2.cloned.1.call-start = ((), (), s32[]{:S(2)}) async-start(), calls=%async_computation.2 | async-start | bytes 14155776 | tf_op jit(solution)/shard_map/reduce_scatter | solution.py:24
  199.3 0.9 copy-start.6
  199.3 1.0 copy-start.5
  272.3 4.9 %collective-permute-start = (bf16[6,3,512]{2,0,1:T(8,128)(2,1)S(1)}, bf16[6,3,512]{2,0,1:T(8,128)(2,1)S(1)}, u32[]{:S(2)}, u32[]{:S(2)}) collective-permute-start(bf16[6,3,512]{2,0,1:T(8,128)(2,1)S(1)} %slice.74), channel_id=1, source_target_pairs={{0,8},{8,16},{16,24},{24,32},{32,40},{40,48},{48,56},{56,64},{64,7... | collective-permute-start | bytes 55304 | tf_op jit(solution)/shard_map/ppermute | solution.py:13
  281.7 1.7 copy-start.2
  359.8 10.5 %copy-start.7 = (f32[16,512]{1,0:T(8,128)S(1)}, f32[16,512]{1,0:T(8,128)}, u32[]{:S(2)}) copy-start(f32[16,512]{1,0:T(8,128)} %get-tuple-element.16) | copy-start | bytes 98308
  359.8 10.5 %copy-start.9 = (pred[8,8]{1,0:T(8,128)(4,1)S(1)}, pred[8,8]{1,0:T(8,128)(4,1)}, u32[]{:S(2)}) copy-start(pred[8,8]{1,0:T(8,128)(4,1)} %fusion.35) | copy-start | bytes 196
  372.8 29.1 %copy-start.3 = (f32[16,512,8]{0,2,1:T(8,128)S(1)}, f32[16,512,8]{0,2,1:T(8,128)}, u32[]{:S(2)}) copy-start(f32[16,512,8]{0,2,1:T(8,128)} %copy.30) | copy-start | bytes 786436
  372.8 29.1 %copy-start.4 = (f32[16,512]{0,1:T(8,128)S(1)}, f32[16,512]{0,1:T(8,128)}, u32[]{:S(2)}) copy-start(f32[16,512]{0,1:T(8,128)} %copy.19) | copy-start | bytes 98308
  406.1 1.7 copy-start.8
  406.1 5.6 %copy-start.1 = (bf16[512,1024]{1,0:T(8,128)(2,1)S(1)}, bf16[512,1024]{1,0:T(8,128)(2,1)}, u32[]{:S(2)}) copy-start(bf16[512,1024]{1,0:T(8,128)(2,1)} %param.6) | copy-start | bytes 3145732
Sparse Core Ops, SparseCore 0:
  9.5 166.0 all-gather.2
  199.4 72.0 reduce-scatter.1
where the time goes:
time: 419 us
  waiting for transfers between devices  242 us (58%)
  matrix products  65.3 us (16%)
  local copies, waits for them, and re-layouts  42.8 us (10%)
  blocking collectives  28.4 us (7%)
  other arithmetic  23.4 us (6%)
  between operations  13.6 us (3%)
    all_gather x1, waiting for transfers between devices, on_device(): lax.all_gather(in_weight, 'ctx', axis=2, tiled=True)  168 us
    reduce_scatter x1, waiting for transfers between devices, on_device(): lax.psum_scatter(partial_value.astype(jnp.bfloat16), 'ch', scatter_dimens...  71.2 us
    gather x2, local copies, waits for them, and re-layouts, on_device(): kernel[jnp.maximum(lag_steps, 0)]  33.1 us
    dot_general x1, matrix products, on_device(): within = jnp.einsum('tsc,jsc->jtc', toeplitz, pieces, precision=highest)  29.1 us
    all_gather x1, blocking collectives, on_device(): lax.all_gather(end_state[None].astype(jnp.bfloat16), 'ctx', axis=0, tiled...  28.4 us
    dot_general x1, matrix products, on_device(): jnp.einsum('td,dmg->tmg', tokens, lax.all_gather(in_weight, 'ctx', axis=2...  23.7 us
  transfers between devices with their start and end apart: 3, of which 3 were waited for; matrix products, arithmetic and copies ran while one was open for 0% of the time, Pallas kernels for 0%

commit v1 on v0

--- a/solution.py
+++ b/solution.py
@@ -5,6 +5,11 @@
 from jax.sharding import PartitionSpec as P
 
 SHORT = 7
+
+
+def gather_over(value, axis, dim):
+    outgoing = jnp.stack([value] * lax.axis_size(axis))
+    return jnp.concatenate(lax.all_to_all(outgoing, axis, 0, 0), axis=dim)
 
 
 def passed_along(value, axis, steps):
@@ -67,9 +72,7 @@
     local_conv = within.reshape(length, channels)
     tail_decay = jnp.exp(-decay_rate[:, None, :] * (length - 1.0 - offsets)[None, :, None])
     end_state = jnp.sum(tail_decay * source[None, :, :], axis=1)
-    states = lax.all_gather(end_state[None].astype(jnp.bfloat16), "ctx", axis=0, tiled=True).astype(
-        jnp.float32
-    )
+    states = gather_over(end_state[None].astype(jnp.bfloat16), "ctx", 0).astype(jnp.float32)
     position = lax.axis_index("ctx")
     earlier_ids = jnp.arange(states.shape[0], dtype=jnp.int32)
     distance = jnp.maximum(position - 1 - earlier_ids, 0).astype(jnp.float32)

time: 419 us -> 400 us (0.955)
  blocking collectives: 28.4 us -> 0 us
  starting transfers between devices: 3.42 us -> 11.1 us
    all_gather x1 -> x0, blocking collectives: 28.4 us -> none  [on_device(): lax.all_gather(end_state[None].astype(jnp.bfloat16), 'ctx', axis=0, tiled...]
    all_to_all x0 -> x1, starting transfers between devices: none -> 7.7 us  [gather_over(): return jnp.concatenate(lax.all_to_all(outgoing, axis, 0, 0), axis=dim)]
  transfers between devices with their start and end apart: 3 -> 4, of which waited for: 3 -> 3; matrix products, arithmetic and copies ran while one was open for 0% -> 3% of each run, Pallas kernels for 0% -> 0%
where the time goes in v1:
time: 400 us; the launch traced here: 399 us
  waiting for transfers between devices  242 us (60%)
  matrix products  65.3 us (16%)
  local copies, waits for them, and re-layouts  44.3 us (11%)
  other arithmetic  22.6 us (6%)
  between operations  13.7 us (3%)
  starting transfers between devices  11.1 us (3%)
    all_gather x1, waiting for transfers between devices, on_device(): lax.all_gather(in_weight, 'ctx', axis=2, tiled=True)  168 us
    reduce_scatter x1, waiting for transfers between devices, on_device(): lax.psum_scatter(partial_value.astype(jnp.bfloat16), 'ch', scatter_dimens...  71.2 us
    gather x2, local copies, waits for them, and re-layouts, on_device(): kernel[jnp.maximum(lag_steps, 0)]  33.1 us
    dot_general x1, matrix products, on_device(): within = jnp.einsum('tsc,jsc->jtc', toeplitz, pieces, precision=highest)  29.1 us
    dot_general x1, matrix products, on_device(): jnp.einsum('td,dmg->tmg', tokens, lax.all_gather(in_weight, 'ctx', axis=2...  23.7 us
    dot_general x1, matrix products, on_device(): block_ends = jnp.einsum('rsc,jsc->jrc', closing, pieces, precision=highest)  8.29 us
  transfers between devices with their start and end apart: 4, of which 3 were waited for; matrix products, arithmetic and copies ran while one was open for 3% of the time, Pallas kernels for 0%

profile of v1, /device:TPU:0, one launch (start us, length us, event | category | flops | bytes accessed | tf_op | source)
XLA Modules:
  0.0 398.5 jit_solution(9055673827298107219)
XLA Ops:
  6.5 0.0 copy-start
  6.5 0.0 all-gather.2.cloned.1.call-start
  6.5 0.7 all-gather.2.cloned.1.call-update
  7.3 0.0 reduce-scatter.2.cloned.1.call-start
  7.3 168.3 %all-gather.2.cloned.1.call-done = bf16[1024,3,4096]{2,0,1:T(8,128)(2,1)} async-done(((bf16[1024,3,256]{2,0,1:T(8,128)(2,1)}), bf16[1024,3,4096]{2,0,1:T(8,128)(2,1)}) %all-gather.2.cloned.1.call-update) | async-done | bytes 25165840 | tf_op jit(solution)/shard_map/all_gather | solution.py:26
  175.6 0.0 copy-done
  175.6 23.7 %convolution_convert_fusion = bf16[512,3,4096]{2,0,1:T(8,128)(2,1)} fusion(bf16[1024,3,4096]{2,0,1:T(8,128)(2,1)} %all-gather.2.cloned.1.call-done, bf16[512,1024]{1,0:T(8,128)(2,1)S(1)} %copy-done), kind=kOutput, calls=%fused_computation.6 | convolution fusion | flops 12891193344 | bytes 38797312 | tf_op jit(solution)/shard_map/td,dmg->tmg/dot_general | solution.py:23
  199.3 0.0 copy-start.7
  199.3 0.0 copy-start.6
  199.3 0.0 reduce-scatter.2.cloned.1.call-update
  199.4 0.1 reshape.143
  199.5 0.7 fusion.35
  200.2 0.1 maximum_convert_fusion.1
  200.3 0.0 copy-done.7
  200.3 0.0 copy-done.6
  200.4 71.2 %reduce-scatter.2.cloned.1.call-done = bf16[512,3,512]{2,0,1:T(8,128)(2,1)} async-done(((bf16[512,3,4096]{2,0,1:T(8,128)(2,1)}), bf16[512,3,512]{2,0,1:T(8,128)(2,1)}) %reduce-scatter.2.cloned.1.call-update) | async-done | bytes 1572880 | tf_op jit(solution)/shard_map/reduce_scatter | solution.py:29
  271.6 0.7 slice.74
  272.3 3.4 collective-permute-start
  275.7 0.1 copy.26
  275.8 1.3 collective-permute-done
  277.2 1.9 maximum_convert_fusion
  279.1 2.6 fusion.10
  281.7 0.0 copy-start.2
  281.7 0.2 fusion.42
  281.9 0.2 slice_multiply_fusion.7
  282.1 1.3 copy-done.2
  283.4 2.9 multiply_reduce_fusion.1
  286.3 0.7 stack.2
  287.0 7.7 %all-to-all-start = ((bf16[16,1,16,512]{3,2,1,0:T(8,128)(2,1)}), bf16[16,1,16,512]{3,2,1,0:T(8,128)(2,1)}, u32[]{:S(2)}, u32[]{:S(2)}) async-start(bf16[16,1,16,512]{3,2,1,0:T(8,128)(2,1)} %stack.2), calls=%async_computation.1 | async-start | bytes 524288 | tf_op jit(solution)/shard_map/all_to_all | solution.py:12
  294.7 0.8 copy.24
  295.5 0.0 copy-start.8
  295.5 8.3 %fusion.22 = f32[16,512,8]{0,2,1:T(8,128)} fusion(f32[8,64,512]{1,0,2:T(8,128)S(1)} %copy.24, f32[64]{0:T(128)S(1)} %iota_subtract_fusion.2, f32[16,512]{0,1:T(8,128)S(1)} %copy.26), kind=kOutput, calls=%fused_computation.36 | convolution fusion | flops 50855936 | bytes 1343744 | tf_op jit(solution)/shard_map/rsc,jsc->jrc/dot_general | solution.py:61
  303.8 2.9 copy.44
  306.7 0.0 all-to-all-done
  306.7 1.1 fusion.34
  307.8 0.0 copy-done.8
  307.8 0.6 fusion.37
  308.5 0.8 copy.25
  309.3 7.8 %multiply_reduce_fusion.2 = (f32[512,512]{1,0:T(8,128)S(1)}, f32[512,512]{1,0:T(8,128)}) fusion(f32[16,512]{1,0:T(8,128)S(1)} %get-tuple-element.8, f32[16,512]{1,0:T(8,128)S(1)} %get-tuple-element.18, f32[16,512]{1,0:T(8,128)} %get-tuple-element.7, f32[512]{0:T(512)S(1)} %iota_add_fusion), kind=kLoop, calls=%fused_computation.5 | loop fusion | flops 24641536 | bytes 2197504 | tf_op jit(solution)/shard_map/reduce_sum | solution.py:48
  317.1 16.8 %gather_fusion = f32[4096,512]{1,0:T(8,128)} fusion(f32[512,512]{1,0:T(8,128)S(1)} %get-tuple-element.5, s32[4096]{0:T(1024)S(1)} %broadcast_clamp_fusion), kind=kCustom, calls=%fused_computation | custom fusion | bytes 16793600 | tf_op jit(solution)/shard_map/gather | solution.py:57
  333.9 0.0 copy-start.5
  333.9 0.0 copy-start.9
  333.9 0.0 copy-start.11
  333.9 16.3 %copy.23 = f32[64,64,512]{1,0,2:T(8,128)} copy(f32[64,64,512]{2,1,0:T(8,128)} %bitcast.56) | data formatting | bytes 16777216 | tf_op jit(solution)/shard_map/gather | solution.py:57
  350.2 0.0 copy-done.5
  350.2 0.0 copy-done.9
  350.2 0.0 copy-done.11
  350.2 0.5 multiply_reduce_fusion.3
  350.8 2.0 copy.36
  352.8 0.0 copy-start.3
  352.8 0.0 copy-start.4
  352.8 29.1 %fusion = f32[512,8,64]{2,1,0:T(8,128)S(1)} fusion(f32[8,64,512]{1,0,2:T(8,128)S(1)} %copy.24, f32[64,64,512]{1,0,2:T(8,128)} %copy.23, pred[64,64]{1,0:T(8,128)(4,1)S(1)} %subtract_compare_fusion), kind=kOutput, calls=%fused_computation.3 | convolution fusion | flops 203423744 | bytes 10489856 | tf_op jit(solution)/shard_map/tsc,jsc->jtc/dot_general | solution.py:58
  381.9 0.0 copy-done.3
  381.9 0.0 copy-done.4
  381.9 4.2 %add_bitcast_fusion = f32[8,64,512]{1,0,2:T(8,128)S(1)} fusion(f32[512,8,64]{2,1,0:T(8,128)S(1)} %fusion, f32[64]{0:T(128)S(1)} %iota_add_fusion.1, f32[16,512]{0,1:T(8,128)S(1)} %copy.26, f32[16,512,8]{0,2,1:T(8,128)S(1)} %copy-done.3, f32[16,512]{0,1:T(8,128)S(1)} %copy-done.4), kind=kOutput, calls=%fused_computation.30 | convolution fusion | flops 51183616 | bytes 2425088 | tf_op jit(solution)/shard_map/rtc,jrc->jtc/dot_general | solution.py:69
  386.1 0.0 copy-start.10
  386.1 0.0 copy-start.1
  386.1 1.7 copy.28
  387.8 0.0 copy-done.10
  387.8 3.9 fusion.30
  391.7 0.0 copy-done.1
  (16 shorter events, 0.1 us)
Async XLA Ops:
  6.5 169.1 %copy-start = (bf16[512,1024]{1,0:T(8,128)(2,1)S(1)}, bf16[512,1024]{1,0:T(8,128)(2,1)}, u32[]{:S(2)}) copy-start(bf16[512,1024]{1,0:T(8,128)(2,1)} %param.6) | copy-start | bytes 3145732
  6.5 169.1 %all-gather.2.cloned.1.call-start = ((), (), s32[]{:S(2)}) async-start(), calls=%async_computation.2 | async-start | bytes 26738688 | tf_op jit(solution)/shard_map/all_gather | solution.py:26
  7.3 264.3 %reduce-scatter.2.cloned.1.call-start = ((), (), s32[]{:S(2)}) async-start(), calls=%async_computation.3 | async-start | bytes 14155776 | tf_op jit(solution)/shard_map/reduce_scatter | solution.py:29
  199.3 0.9 copy-start.7
  199.3 1.0 copy-start.6
  272.3 4.9 %collective-permute-start = (bf16[6,3,512]{2,0,1:T(8,128)(2,1)S(1)}, bf16[6,3,512]{2,0,1:T(8,128)(2,1)S(1)}, u32[]{:S(2)}, u32[]{:S(2)}) collective-permute-start(bf16[6,3,512]{2,0,1:T(8,128)(2,1)S(1)} %slice.74), channel_id=1, source_target_pairs={{0,8},{8,16},{16,24},{24,32},{32,40},{40,48},{48,56},{56,64},{64,7... | collective-permute-start | bytes 55304 | tf_op jit(solution)/shard_map/ppermute | solution.py:18
  281.7 1.7 copy-start.2
  287.0 19.6 %all-to-all-start = ((bf16[16,1,16,512]{3,2,1,0:T(8,128)(2,1)}), bf16[16,1,16,512]{3,2,1,0:T(8,128)(2,1)}, u32[]{:S(2)}, u32[]{:S(2)}) async-start(bf16[16,1,16,512]{3,2,1,0:T(8,128)(2,1)} %stack.2), calls=%async_computation.1 | async-start | bytes 524288 | tf_op jit(solution)/shard_map/all_to_all | solution.py:12
  295.5 12.3 %copy-start.8 = (f32[16,512]{1,0:T(8,128)S(1)}, f32[16,512]{1,0:T(8,128)}, u32[]{:S(2)}) copy-start(f32[16,512]{1,0:T(8,128)} %param.9) | copy-start | bytes 98308
  333.9 16.3 %copy-start.5 = (f32[16,512,8]{1,0,2:T(8,128)S(1)}, f32[16,512,8]{1,0,2:T(8,128)}, u32[]{:S(2)}) copy-start(f32[16,512,8]{1,0,2:T(8,128)} %copy.44) | copy-start | bytes 786436
  333.9 16.3 %copy-start.9 = (f32[16,512]{1,0:T(8,128)S(1)}, f32[16,512]{1,0:T(8,128)}, u32[]{:S(2)}) copy-start(f32[16,512]{1,0:T(8,128)} %get-tuple-element.16) | copy-start | bytes 98308
  333.9 16.3 %copy-start.11 = (pred[8,8]{1,0:T(8,128)(4,1)S(1)}, pred[8,8]{1,0:T(8,128)(4,1)}, u32[]{:S(2)}) copy-start(pred[8,8]{1,0:T(8,128)(4,1)} %fusion.35) | copy-start | bytes 196
  352.8 29.1 %copy-start.3 = (f32[16,512,8]{0,2,1:T(8,128)S(1)}, f32[16,512,8]{0,2,1:T(8,128)}, u32[]{:S(2)}) copy-start(f32[16,512,8]{0,2,1:T(8,128)} %copy.36) | copy-start | bytes 786436
  352.8 29.1 %copy-start.4 = (f32[16,512]{0,1:T(8,128)S(1)}, f32[16,512]{0,1:T(8,128)}, u32[]{:S(2)}) copy-start(f32[16,512]{0,1:T(8,128)} %copy.25) | copy-start | bytes 98308
  386.1 1.7 copy-start.10
  386.1 5.6 %copy-start.1 = (bf16[512,1024]{1,0:T(8,128)(2,1)S(1)}, bf16[512,1024]{1,0:T(8,128)(2,1)}, u32[]{:S(2)}) copy-start(bf16[512,1024]{1,0:T(8,128)(2,1)} %param.6) | copy-start | bytes 3145732
Sparse Core Ops, SparseCore 0:
  9.5 166.0 all-gather.1
  199.5 72.0 reduce-scatter.1
